TPU v7x, 32 devices: a whole 2x2x4 slice. The times are simulated.
32 devices in a mesh: front: 8 (over z, y), pair: 4 (over x, core).
Axes of the slice: x: 2, y: 2, z: 4, core: 2. Of those that a mesh axis runs over, the one named last changes fastest.
Arguments:
- pivot_block: float32 [8, 768, 768], P('front', 'pair'), may hold values from -1 to 8, as said below
- coupling_rows: float32 [8, 2304, 768], P('front', 'pair'), may hold values from -0.6 to 0.6
- trailing_block: float32 [8, 2304, 2304], P('front', 'pair'), may hold values from -6 to 6
- index_map: int32 [8, 2304], replicated, may hold values from 0 to 3071, as said below
Outputs:
- panel_factor: float32 [8, 2304, 768], P('front', 'pair')
- parent_front: float32 [3072, 8, 768], P('pair', 'front')
Inputs may be any that keep to these rules, and one draw needn't show every extreme that they name: pivot_block[c] is symmetric positive definite. For each child c and row block p, the entries index_map[c, p * 576 + a] for a below 576 are distinct, rising, and lie in p * 768 to (p + 1) * 768 - 1.
All inputs are finite; a program needn't handle non-finite values.
Results may differ from a plain program's by a relative error of at most 0.0029.
Values may be sent and summed in bfloat16 or wider, within the bound.
A program may use at most 128 MiB of HBM per device.

v0:
```python
import jax
import jax.numpy as jnp
from jax import lax
from jax.experimental import pallas as pl
from jax.experimental.pallas import tpu as pltpu
from jax.sharding import PartitionSpec as P

PO = 3072
SIBLINGS = 4
BLK = 128
SUB = 8


def dot_t(a, b):
    return lax.dot_general(a, b, (((1,), (1,)), ((), ())), preferred_element_type=jnp.float32)


def halves(value):
    high = value.astype(jnp.bfloat16)
    return high, (value - high.astype(jnp.float32)).astype(jnp.bfloat16)


def dot3(a, b):
    return dot_t(a[0], b[0]) + (dot_t(a[0], b[1]) + dot_t(a[1], b[0]))


def inverse_factor(block):
    size = block.shape[0]
    sub = lax.broadcasted_iota(jnp.int32, (SUB, size), 0)
    lane = lax.broadcasted_iota(jnp.int32, (SUB, size), 1)
    rest = block
    done = []
    for start in range(0, size, SUB):
        rows = size - start
        cols = [
            jnp.broadcast_to(rest[:, start + j : start + j + 1], (rows, size)) for j in range(SUB)
        ]
        rest_lane = lax.broadcasted_iota(jnp.int32, (rows, size), 1)
        rest = jnp.where((rest_lane >= start) & (rest_lane < start + SUB), 0.0, rest)
        slab = jnp.where(lane - start == sub, 1.0, rest[:SUB])
        top = [c[:SUB] for c in cols]
        more = rows > SUB
        if more:
            below = rest[SUB:]
            low = [c[SUB:] for c in cols]
        scale = jnp.ones((SUB, size), jnp.float32)
        for t in range(SUB):
            pivot = top[t][t : t + 1, :]
            recip = 1.0 / pivot
            scale = jnp.where(sub == t, lax.rsqrt(pivot), scale)
            for j in range(t + 1, SUB):
                mult = top[j][t : t + 1, :] * recip
                top[j] = top[j] - top[t] * mult
                if more:
                    low[j] = low[j] - low[t] * mult
            row = slab[t : t + 1, :] * recip
            slab = slab - jnp.where(sub > t, top[t], 0.0) * row
            if more:
                below = below - low[t] * row
        done.append(slab * scale)
        if more:
            rest = below
    whole = jnp.concatenate(done, axis=0)
    row_id = lax.broadcasted_iota(jnp.int32, (size, size), 0)
    col_id = lax.broadcasted_iota(jnp.int32, (size, size), 1)
    return jnp.where(col_id <= row_id, whole, 0.0)


def factor_kernel(pivot_ref, coupling_ref, factor_ref, half_ref, work, rows_left):
    order = pivot_ref.shape[0]
    work[...] = pivot_ref[...]
    rows_left[...] = coupling_ref[...]

    def step(k, carry):
        at = pl.ds(pl.multiple_of(k * BLK, BLK), BLK)
        inverse = halves(inverse_factor(work[at, at]))
        panel = halves(dot3(halves(work[:, at]), inverse))
        solved = dot3(halves(rows_left[:, at]), inverse)
        factor_ref[:, at] = solved
        half_ref[:, at] = solved.astype(jnp.bfloat16)
        solved = halves(solved)
        for c in range(0, order, 256):
            cs = slice(c, c + 256)
            part = (panel[0][cs], panel[1][cs])
            work[:, cs] = work[:, cs] - dot3(panel, part)
            rows_left[:, cs] = rows_left[:, cs] - dot3(solved, part)
        return carry

    lax.fori_loop(0, order // BLK, step, 0)


def factor_rows(pivot, coupling):
    order = pivot.shape[0]
    rows = coupling.shape[0]
    return pl.pallas_call(
        factor_kernel,
        out_shape=(
            jax.ShapeDtypeStruct((rows, order), jnp.float32),
            jax.ShapeDtypeStruct((rows, order), jnp.bfloat16),
        ),
        in_specs=[pl.BlockSpec(memory_space=pltpu.VMEM)] * 2,
        out_specs=[pl.BlockSpec(memory_space=pltpu.VMEM)] * 2,
        scratch_shapes=[
            pltpu.VMEM((order, order), jnp.float32),
            pltpu.VMEM((rows, order), jnp.float32),
        ],
        compiler_params=pltpu.CompilerParams(vmem_limit_bytes=48 * 2**20),
    )(pivot, coupling)


def body(pivot_block, coupling_rows, trailing_block, index_map):
    child_id = lax.axis_index("front")
    pair_id = lax.axis_index("pair")
    pairs = lax.axis_size("pair")
    fronts = lax.axis_size("front")
    whole_pivot = lax.all_gather(pivot_block[0], "pair", axis=0, tiled=True)
    factor, panel_half = factor_rows(whole_pivot, coupling_rows[0])
    whole_half = lax.all_gather(panel_half, "pair", axis=0, tiled=True)
    upd_rows = panel_half.shape[0]
    upd_cols = trailing_block.shape[2] // SIBLINGS
    row_count = PO // pairs
    col_count = PO // SIBLINGS
    sibling = child_id % SIBLINGS

    def piece(block):
        there = lax.dynamic_slice_in_dim(whole_half, block * upd_cols, upd_cols)
        old = lax.dynamic_slice_in_dim(trailing_block[0], block * upd_cols, upd_cols, axis=1)
        return (old - dot_t(panel_half, there)).astype(jnp.bfloat16)

    pieces = []
    for apart in (3, 1, 2):
        mine = piece(sibling ^ apart)
        pieces.append(
            (apart, lax.ppermute(mine, "front", [(i, i ^ apart) for i in range(fronts)]))
        )
    pieces.append((0, piece(sibling)))

    assembled = jnp.zeros((row_count, col_count), jnp.float32)
    for apart, value in pieces:
        child_map = lax.dynamic_index_in_dim(index_map, child_id ^ apart, 0, keepdims=False)
        rows_map = lax.dynamic_slice_in_dim(child_map, pair_id * upd_rows, upd_rows)
        cols_map = lax.dynamic_slice_in_dim(child_map, sibling * upd_cols, upd_cols)
        row_hot = (
            rows_map[None, :] - pair_id * row_count == jnp.arange(row_count, dtype=jnp.int32)[:, None]
        ).astype(jnp.bfloat16)
        col_hot = (
            cols_map[:, None] - sibling * col_count == jnp.arange(col_count, dtype=jnp.int32)[None, :]
        ).astype(jnp.bfloat16)
        moved = jnp.dot(value, col_hot, preferred_element_type=jnp.float32).astype(jnp.bfloat16)
        assembled = assembled + jnp.dot(row_hot, moved, preferred_element_type=jnp.float32)
    return (factor[None, :, :], assembled[:, None, :])


def solution(mesh):
    in_specs = (P("front", "pair", None), P("front", "pair", None), P("front", "pair", None), P())
    out_specs = (P("front", "pair", None), P("pair", "front", None))
    return jax.shard_map(body, mesh=mesh, in_specs=in_specs, out_specs=out_specs, check_vma=False)
```

profile of v0, /device:TPU:0, one launch (start us, length us, event | category | flops | bytes accessed | tf_op | source)
XLA Modules:
  0.0 169.3 jit_solution(9313480498011438891)
XLA Ops:
  7.2 0.0 all-gather.6.cloned.1.call-start
  7.2 0.7 all-gather.6.cloned.1.call-update
  7.9 0.0 all-gather.4.cloned.1.call-start
  7.9 28.4 %all-gather.6.cloned.1.call-done = f32[1,768,768]{2,1,0:T(8,128)} async-done(((f32[1,192,768]{2,1,0:T(8,128)}), f32[1,768,768]{2,1,0:T(8,128)}) %all-gather.6.cloned.1.call-update) | async-done | bytes 2359312 | tf_op jit(solution)/shard_map/all_gather | solution.py:116
  36.4 1.7 copy-done
  38.0 1.5 copy-done.1
  39.5 32.8 %shard_map.59 = (f32[576,768]{1,0:T(8,128)}, bf16[576,768]{1,0:T(8,128)(2,1)}) custom-call(f32[768,768]{1,0:T(8,128)S(1)} %bitcast.31, f32[576,768]{1,0:T(8,128)S(1)} %bitcast.32), custom_call_target="tpu_custom_call" | custom-call | tf_op jit(solution)/shard_map/pallas_call | solution.py:95
  72.4 1.2 subtract_reduce_fusion.1
  73.6 29.7 %all-gather.4.cloned.1.call-done = bf16[2304,768]{1,0:T(8,128)(2,1)} async-done(((bf16[576,768]{1,0:T(8,128)(2,1)}), bf16[2304,768]{1,0:T(8,128)(2,1)}) %all-gather.4.cloned.1.call-update) | async-done | bytes 3538960 | tf_op jit(solution)/shard_map/all_gather | solution.py:118
  103.3 3.0 %fusion.9 = bf16[576,576]{1,0:T(8,128)(2,1)S(1)} fusion(f32[1,576,2304]{2,1,0:T(8,128)} %param.6, s32[]{:T(128)S(6)} %select_n.71, bf16[576,768]{1,0:T(8,128)(2,1)} %get-tuple-element.5, bf16[2304,768]{1,0:T(8,128)(2,1)} %all-gather.4.cloned.1.call-done), kind=kOutput, calls=%fused_computation.20 | convolution fusion | flops 510271488 | bytes 3908608 | tf_op jit(solution)/shard_map/dot_general | solution.py:15
  106.3 1.5 collective-permute-start.2
  107.9 3.5 %fusion.10 = bf16[576,576]{1,0:T(8,128)(2,1)} fusion(f32[1,576,2304]{2,1,0:T(8,128)} %param.6, s32[]{:T(128)S(6)} %select_n.68, bf16[576,768]{1,0:T(8,128)(2,1)} %get-tuple-element.5, bf16[2304,768]{1,0:T(8,128)(2,1)S(1)} %copy-done.2), kind=kOutput, calls=%fused_computation.22 | convolution fusion | flops 510271488 | bytes 3761152 | tf_op jit(solution)/shard_map/dot_general | solution.py:15
  111.4 1.5 collective-permute-start.1
  112.9 3.4 %fusion.11 = bf16[576,576]{1,0:T(8,128)(2,1)} fusion(f32[1,576,2304]{2,1,0:T(8,128)} %param.6, s32[]{:T(128)S(6)} %select_n.63, bf16[576,768]{1,0:T(8,128)(2,1)} %get-tuple-element.5, bf16[2304,768]{1,0:T(8,128)(2,1)S(1)} %copy-done.2), kind=kOutput, calls=%fused_computation.24 | convolution fusion | flops 510271488 | bytes 3761152 | tf_op jit(solution)/shard_map/dot_general | solution.py:15
  116.3 0.5 collective-permute-start
  116.8 3.7 %fusion.12 = bf16[576,768]{1,0:T(8,128)(2,1)S(1)} fusion(f32[1,576,2304]{2,1,0:T(8,128)} %param.6, s32[]{:T(128)S(6)} %select_n.64, bf16[576,768]{1,0:T(8,128)(2,1)} %get-tuple-element.5, s32[576]{0:T(1024)S(1)} %get-tuple-element.15, bf16[2304,768]{1,0:T(8,128)(2,1)} %all-gather.4.cloned.1.call-done), kind=kOutput, calls=%fused_computation.25 | convolution fusion | flops 1020764160 | bytes 4132096 | tf_op jit(solution)/shard_map/dot_general | solution.py:149
  120.6 5.2 %collective-permute-done.2 = bf16[576,576]{1,0:T(8,128)(2,1)S(1)} collective-permute-done((bf16[576,576]{1,0:T(8,128)(2,1)S(1)}, bf16[576,576]{1,0:T(8,128)(2,1)S(1)}, u32[]{:S(2)}, u32[]{:S(2)}) %collective-permute-start.2) | collective-permute-done | bytes 663584 | tf_op jit(solution)/shard_map/ppermute | solution.py:134
  125.7 0.9 copy-done.3
  126.6 3.1 %fusion.2 = f32[768,768]{1,0:T(8,128)S(1)} fusion(bf16[576,576]{1,0:T(8,128)(2,1)} %copy-done.3, s32[576]{0:T(1024)S(1)} %get-tuple-element.10, s32[576]{0:T(1024)S(1)} %get-tuple-element.9), kind=kOutput, calls=%fused_computation.7 | convolution fusion | flops 1190412288 | bytes 3027456 | tf_op jit(solution)/shard_map/dot_general | solution.py:150
  129.7 16.2 %collective-permute-done.1 = bf16[576,576]{1,0:T(8,128)(2,1)} collective-permute-done((bf16[576,576]{1,0:T(8,128)(2,1)}, bf16[576,576]{1,0:T(8,128)(2,1)}, u32[]{:S(2)}, u32[]{:S(2)}) %collective-permute-start.1) | collective-permute-done | bytes 663584 | tf_op jit(solution)/shard_map/ppermute | solution.py:134
  145.9 4.5 %fusion.1 = f32[768,768]{1,0:T(8,128)} fusion(bf16[576,576]{1,0:T(8,128)(2,1)} %collective-permute-done.1, s32[576]{0:T(1024)S(1)} %get-tuple-element.12, s32[576]{0:T(1024)S(1)} %get-tuple-element.11), kind=kOutput, calls=%fused_computation.6 | convolution fusion | flops 1190412288 | bytes 3027456 | tf_op jit(solution)/shard_map/dot_general | solution.py:150
  150.4 4.5 %fusion = f32[768,768]{1,0:T(8,128)} fusion(bf16[576,576]{1,0:T(8,128)(2,1)} %collective-permute-done, s32[576]{0:T(1024)S(1)} %get-tuple-element.14, s32[576]{0:T(1024)S(1)} %get-tuple-element.13), kind=kOutput, calls=%fused_computation.5 | convolution fusion | flops 1190412288 | bytes 3027456 | tf_op jit(solution)/shard_map/dot_general | solution.py:150
  155.0 3.6 %add_bitcast_fusion = f32[768,1,768]{2,0,1:T(8,128)S(1)} fusion(f32[768,768]{1,0:T(8,128)S(1)} %fusion.2, f32[768,768]{1,0:T(8,128)} %fusion, f32[768,768]{1,0:T(8,128)} %fusion.1, bf16[576,768]{1,0:T(8,128)(2,1)S(1)} %fusion.12, s32[576]{0:T(1024)S(1)} %get-tuple-element.8), kind=kOutput, calls=%fused_computation | convolution fusion | flops 681689088 | bytes 10324224 | tf_op jit(solution)/shard_map/dot_general | solution.py:150
  158.6 3.8 %copy.6 = f32[768,1,768]{2,1,0:T(1,128)} copy(f32[768,1,768]{2,0,1:T(8,128)S(1)} %add_bitcast_fusion) | data formatting | bytes 4718592
  (7 shorter events, 0.0 us)
Async XLA Ops:
  7.2 29.2 %all-gather.6.cloned.1.call-start = ((), (), s32[]{:S(2)}) async-start(), calls=%async_computation.1 | async-start | bytes 2949120 | tf_op jit(solution)/shard_map/all_gather | solution.py:116
  7.9 95.4 %all-gather.4.cloned.1.call-start = ((), (), s32[]{:S(2)}) async-start(), calls=%async_computation | async-start | bytes 4423680 | tf_op jit(solution)/shard_map/all_gather | solution.py:118
  36.4 1.7 copy-start
  38.0 1.5 copy-start.1
  103.3 4.6 %copy-start.2 = (bf16[2304,768]{1,0:T(8,128)(2,1)S(1)}, bf16[2304,768]{1,0:T(8,128)(2,1)}, u32[]{:S(2)}) copy-start(bf16[2304,768]{1,0:T(8,128)(2,1)} %all-gather.4.cloned.1.call-done) | copy-start | bytes 10616836
  106.3 19.4 %collective-permute-start.2 = (bf16[576,576]{1,0:T(8,128)(2,1)S(1)}, bf16[576,576]{1,0:T(8,128)(2,1)S(1)}, u32[]{:S(2)}, u32[]{:S(2)}) collective-permute-start(bf16[576,576]{1,0:T(8,128)(2,1)S(1)} %fusion.9), channel_id=1, source_target_pairs={{0,8},{4,12},{8,0},{12,4},{16,24},{20,28},{24,16},{28,20},{1,9},{5... | collective-permute-start | bytes 1990664 | tf_op jit(solution)/shard_map/ppermute | solution.py:134
  111.4 34.5 %collective-permute-start.1 = (bf16[576,576]{1,0:T(8,128)(2,1)}, bf16[576,576]{1,0:T(8,128)(2,1)}, u32[]{:S(2)}, u32[]{:S(2)}) collective-permute-start(bf16[576,576]{1,0:T(8,128)(2,1)} %fusion.10), channel_id=1, source_target_pairs={{0,4},{4,0},{8,12},{12,8},{16,20},{20,16},{24,28},{28,24},{1,5},{5... | collective-permute-start | bytes 1990664 | tf_op jit(solution)/shard_map/ppermute | solution.py:134
  116.3 34.1 %collective-permute-start = (bf16[576,576]{1,0:T(8,128)(2,1)}, bf16[576,576]{1,0:T(8,128)(2,1)}, u32[]{:S(2)}, u32[]{:S(2)}) collective-permute-start(bf16[576,576]{1,0:T(8,128)(2,1)} %fusion.11), channel_id=1, source_target_pairs={{0,12},{4,8},{8,4},{12,0},{16,28},{20,24},{24,20},{28,16},{1,13},{... | collective-permute-start | bytes 1990664 | tf_op jit(solution)/shard_map/ppermute | solution.py:134
  125.7 0.9 copy-start.3
Sparse Core Ops, SparseCore 0:
  9.6 26.7 all-gather.5
  72.5 30.7 all-gather.3
where the time goes:
time: 170 us; the launch traced here: 169 us
  waiting for transfers between devices  80.1 us (47%)
  Pallas kernels  32.8 us (19%)
  matrix products  29.5 us (17%)
  between operations  14.2 us (8%)
  local copies, waits for them, and re-layouts  7.84 us (5%)
  starting transfers between devices  3.63 us (2%)
    pallas_call x1, Pallas kernels, factor_rows(): pl.pallas_call(factor_kernel, out_shape=(jax.ShapeDtypeStruct((rows, orde...  32.8 us
    all_gather x1, waiting for transfers between devices, body(): whole_half = lax.all_gather(panel_half, 'pair', axis=0, tiled=True)  29.7 us
    all_gather x1, waiting for transfers between devices, body(): whole_pivot = lax.all_gather(pivot_block[0], 'pair', axis=0, tiled=True)  28.4 us
    ppermute x3, waiting for transfers between devices, body(): lax.ppermute(mine, 'front', [(i, i ^ apart) for i in range(fronts)])  21.3 us
    dot_general x4, matrix products, body(): jnp.dot(row_hot, moved, preferred_element_type=jnp.float32)  15.8 us
    dot_general x3, matrix products, dot_t(): lax.dot_general(a, b, (((1,), (1,)), ((), ())), preferred_element_type=jn...  9.98 us
    unnamed x9, local copies, waits for them, and re-layouts  7.84 us
    dot_general x1, matrix products, body(): jnp.dot(value, col_hot, preferred_element_type=jnp.float32)  3.72 us
  transfers between devices with their start and end apart: 5, of which 4 were waited for; matrix products, arithmetic and copies ran while one was open for 12% of the time, Pallas kernels for 0%

commit v1 on v0

v1 whole, which is shorter than its diff:
```python
import jax
import jax.numpy as jnp
from jax import lax
from jax.experimental import pallas as pl
from jax.experimental.pallas import tpu as pltpu
from jax.sharding import PartitionSpec as P

PO = 3072
SIBLINGS = 4
BLK = 128
SUB = 8
MESH = pl.DeviceIdType.MESH


def dot_t(a, b):
    return lax.dot_general(a, b, (((1,), (1,)), ((), ())), preferred_element_type=jnp.float32)


def halves(value):
    high = value.astype(jnp.bfloat16)
    return high, (value - high.astype(jnp.float32)).astype(jnp.bfloat16)


def dot3(a, b):
    return dot_t(a[0], b[0]) + (dot_t(a[0], b[1]) + dot_t(a[1], b[0]))


def inverse_factor(block):
    size = block.shape[0]
    sub = lax.broadcasted_iota(jnp.int32, (SUB, size), 0)
    lane = lax.broadcasted_iota(jnp.int32, (SUB, size), 1)
    rest = block
    done = []
    for start in range(0, size, SUB):
        rows = size - start
        cols = [
            jnp.broadcast_to(rest[:, start + j : start + j + 1], (rows, size)) for j in range(SUB)
        ]
        rest_lane = lax.broadcasted_iota(jnp.int32, (rows, size), 1)
        rest = jnp.where((rest_lane >= start) & (rest_lane < start + SUB), 0.0, rest)
        slab = jnp.where(lane - start == sub, 1.0, rest[:SUB])
        top = [c[:SUB] for c in cols]
        more = rows > SUB
        if more:
            below = rest[SUB:]
            low = [c[SUB:] for c in cols]
        scale = jnp.ones((SUB, size), jnp.float32)
        for t in range(SUB):
            pivot = top[t][t : t + 1, :]
            recip = 1.0 / pivot
            scale = jnp.where(sub == t, lax.rsqrt(pivot), scale)
            for j in range(t + 1, SUB):
                mult = top[j][t : t + 1, :] * recip
                top[j] = top[j] - top[t] * mult
                if more:
                    low[j] = low[j] - low[t] * mult
            row = slab[t : t + 1, :] * recip
            slab = slab - jnp.where(sub > t, top[t], 0.0) * row
            if more:
                below = below - low[t] * row
        done.append(slab * scale)
        if more:
            rest = below
    whole = jnp.concatenate(done, axis=0)
    row_id = lax.broadcasted_iota(jnp.int32, (size, size), 0)
    col_id = lax.broadcasted_iota(jnp.int32, (size, size), 1)
    return jnp.where(col_id <= row_id, whole, 0.0)


def fused_kernel(
    maps_ref, pivot_ref, coupling_ref, trailing_ref, factor_ref, front_ref,
    raw, work, rows_left, panels, old_flat, old, outgoing, incoming,
    old_sem, piv_send, piv_recv, pan_send, pan_recv, upd_send, upd_recv,
):
    order = pivot_ref.shape[1]
    own_rows = pivot_ref.shape[0]
    upd = coupling_ref.shape[0]
    blocks = order // BLK
    child = lax.axis_index("front")
    me = lax.axis_index("pair")
    sibling = lax.rem(child, SIBLINGS)
    sib_hi, sib_lo = lax.div(sibling, 2), lax.rem(sibling, 2)
    chip, core = lax.div(me, 2), lax.rem(me, 2)
    across = (1 - chip) * 2 + core
    mate = chip * 2 + (1 - core)
    mate_across = (1 - chip) * 2 + (1 - core)

    def relative(apart):
        hi = 1 - sib_hi if apart >= 2 else sib_hi
        lo = 1 - sib_lo if apart % 2 else sib_lo
        return hi * 2 + lo

    def sib_child(apart):
        return child - sibling + relative(apart)

    barrier = pltpu.get_barrier_semaphore()
    for peer in (across, mate):
        pl.semaphore_signal(barrier, inc=1, device_id={"pair": peer}, device_id_type=MESH)
    for apart in (1, 2, 3):
        pl.semaphore_signal(
            barrier, inc=1, device_id={"front": sib_child(apart)}, device_id_type=MESH
        )
    load_old = pltpu.make_async_copy(trailing_ref, old_flat, old_sem)
    load_old.start()
    pl.semaphore_wait(barrier, 5)

    def cols(k):
        return pl.ds(pl.multiple_of(k * BLK, BLK), BLK)

    def pivot_rows(owner):
        return pl.ds(pl.multiple_of(owner * own_rows, 8), own_rows)

    def pivot_copy(kind, k, owner, peer):
        spot = raw.at[pivot_rows(owner), cols(k)]
        return pltpu.make_async_remote_copy(
            src_ref=spot if kind == 2 else pivot_ref.at[:, cols(k)],
            dst_ref=spot,
            send_sem=piv_send.at[kind, k],
            recv_sem=piv_recv.at[kind, k],
            device_id={"pair": peer},
            device_id_type=MESH,
        )

    def panel_copy(kind, k, owner, peer):
        spot = panels.at[owner, :, cols(k)]
        return pltpu.make_async_remote_copy(
            src_ref=spot,
            dst_ref=spot,
            send_sem=pan_send.at[kind, k],
            recv_sem=pan_recv.at[kind, k],
            device_id={"pair": peer},
            device_id_type=MESH,
        )

    def relay(copy, k):
        copy(0, k, across, across).wait_recv()
        copy(2, k, across, mate).start()

    for k in range(blocks):
        pivot_copy(0, k, me, across).start()
        pivot_copy(1, k, me, mate).start()

    raw[pivot_rows(me), :] = pivot_ref[...]
    rows_left[...] = coupling_ref[...]
    work[...] = jnp.zeros_like(work)
    load_old.wait()
    for b in range(SIBLINGS):
        old[b] = old_flat[:, b * upd : (b + 1) * upd]
    relay(pivot_copy, 0)

    row_id = lax.broadcasted_iota(jnp.int32, (order, BLK), 0)

    def step(k, carry):
        at = cols(k)
        pivot_copy(1, k, mate, mate).wait_recv()
        pivot_copy(2, k, mate_across, mate).wait_recv()
        inverse = halves(inverse_factor(raw[at, at] + work[at, at]))

        @pl.when(k + 1 < blocks)
        def _():
            relay(pivot_copy, k + 1)

        @pl.when(k > 0)
        def _():
            relay(panel_copy, k - 1)

        solved = dot3(halves(rows_left[:, at]), inverse)
        factor_ref[:, at] = solved
        panels[me, :, at] = solved.astype(jnp.bfloat16)
        panel_copy(0, k, me, across).start()
        panel_copy(1, k, me, mate).start()
        column = jnp.where(row_id >= k * BLK, raw[:, at] + work[:, at], 0.0)
        panel = halves(dot3(halves(column), inverse))
        solved = halves(solved)
        for c in range(0, order, 256):
            cs = slice(c, c + 256)
            part = (panel[0][cs], panel[1][cs])
            work[:, cs] = work[:, cs] - dot3(panel, part)
            rows_left[:, cs] = rows_left[:, cs] - dot3(solved, part)
        return carry

    lax.fori_loop(0, blocks, step, 0)
    relay(panel_copy, blocks - 1)
    for k in range(blocks):
        panel_copy(1, k, mate, mate).wait_recv()
        panel_copy(2, k, mate_across, mate).wait_recv()

    def update_copy(apart):
        return pltpu.make_async_remote_copy(
            src_ref=outgoing.at[apart],
            dst_ref=incoming.at[apart - 1],
            send_sem=upd_send.at[apart],
            recv_sem=upd_recv.at[apart],
            device_id={"front": sib_child(apart)},
            device_id_type=MESH,
        )

    for apart in (3, 1, 2, 0):
        there = relative(apart)
        outgoing[apart] = (old[there] - dot_t(panels[me], panels[there])).astype(jnp.bfloat16)
        if apart:
            update_copy(apart).start()

    row_count, col_count = front_ref.shape
    target_rows = lax.broadcasted_iota(jnp.int32, (row_count, upd), 0)
    target_cols = lax.broadcasted_iota(jnp.int32, (col_count, upd), 0)
    for apart in (0, 1, 2, 3):
        if apart:
            update_copy(apart).wait_recv()
            value = incoming[apart - 1]
        else:
            value = outgoing[0]
        base = sib_child(apart) * SIBLINGS
        rows_map = maps_ref[pl.ds(base + me, 1), :] - me * row_count
        cols_map = maps_ref[pl.ds(base + sibling, 1), :] - sibling * col_count
        row_hot = jnp.where(target_rows == rows_map, 1.0, 0.0).astype(jnp.bfloat16)
        col_hot = jnp.where(target_cols == cols_map, 1.0, 0.0).astype(jnp.bfloat16)
        moved = dot_t(value, col_hot).astype(jnp.bfloat16)
        placed = jnp.dot(row_hot, moved, preferred_element_type=jnp.float32)
        if apart:
            front_ref[...] += placed
        else:
            front_ref[...] = placed

    for k in range(blocks):
        for kind, owner, peer in ((0, me, across), (1, me, mate), (2, across, mate)):
            pivot_copy(kind, k, owner, peer).wait_send()
            panel_copy(kind, k, owner, peer).wait_send()
    for apart in (1, 2, 3):
        update_copy(apart).wait_send()


def body(pivot_block, coupling_rows, trailing_block, index_map):
    pairs = lax.axis_size("pair")
    own_rows, order = pivot_block.shape[1:]
    upd, upd_all = trailing_block.shape[1:]
    blocks = order // BLK
    row_count, col_count = PO // pairs, PO // SIBLINGS
    maps = index_map.reshape(-1, upd)
    vmem = pl.BlockSpec(memory_space=pltpu.VMEM)
    factor, front = pl.pallas_call(
        fused_kernel,
        out_shape=(
            jax.ShapeDtypeStruct((upd, order), jnp.float32),
            jax.ShapeDtypeStruct((row_count, col_count), jnp.float32),
        ),
        in_specs=[vmem, vmem, vmem, pl.BlockSpec(memory_space=pl.ANY)],
        out_specs=[vmem, vmem],
        scratch_shapes=[
            pltpu.VMEM((order, order), jnp.float32),
            pltpu.VMEM((order, order), jnp.float32),
            pltpu.VMEM((upd, order), jnp.float32),
            pltpu.VMEM((pairs, upd, order), jnp.bfloat16),
            pltpu.VMEM((upd, upd_all), jnp.float32),
            pltpu.VMEM((SIBLINGS, upd, upd), jnp.float32),
            pltpu.VMEM((SIBLINGS, upd, upd), jnp.bfloat16),
            pltpu.VMEM((SIBLINGS - 1, upd, upd), jnp.bfloat16),
            pltpu.SemaphoreType.DMA,
            pltpu.SemaphoreType.DMA((3, blocks)),
            pltpu.SemaphoreType.DMA((3, blocks)),
            pltpu.SemaphoreType.DMA((3, blocks)),
            pltpu.SemaphoreType.DMA((3, blocks)),
            pltpu.SemaphoreType.DMA((SIBLINGS,)),
            pltpu.SemaphoreType.DMA((SIBLINGS,)),
        ],
        compiler_params=pltpu.CompilerParams(
            collective_id=0, has_side_effects=True, vmem_limit_bytes=56 * 2**20
        ),
    )(maps, pivot_block[0], coupling_rows[0], trailing_block[0])
    return (factor[None, :, :], front[:, None, :])


def solution(mesh):
    in_specs = (P("front", "pair", None), P("front", "pair", None), P("front", "pair", None), P())
    out_specs = (P("front", "pair", None), P("pair", "front", None))
    return jax.shard_map(body, mesh=mesh, in_specs=in_specs, out_specs=out_specs, check_vma=False)
```

time: 170 us -> 104 us (0.61)
  waiting for transfers between devices: 80.1 us -> 0 us
  Pallas kernels: 32.8 us -> 94.7 us
  matrix products: 29.5 us -> 0 us
  between operations: 14.2 us -> 0.65 us
  starting transfers between devices: 3.63 us -> 0 us
    pallas_call x1, Pallas kernels: 32.8 us -> 94.7 us  [body(): pl.pallas_call(fused_kernel, out_shape=(jax.ShapeDtypeStruct((upd, order)...]
    all_gather x2 -> x0, waiting for transfers between devices: 58.1 us -> none  [the longest x1 29.7 us: body(): whole_half = lax.all_gather(panel_half, 'pair', axis=0, tiled=True)]
    dot_general x8 -> x0, matrix products: 29.5 us -> none  [the longest x4 15.8 us: body(): jnp.dot(row_hot, moved, preferred_element_type=jnp.float32)]
    ppermute x3 -> x0, waiting for transfers between devices: 21.3 us -> none  [body(): lax.ppermute(mine, 'front', [(i, i ^ apart) for i in range(fronts)])]
    ppermute x3 -> x0, starting transfers between devices: 3.56 us -> none  [body(): lax.ppermute(mine, 'front', [(i, i ^ apart) for i in range(fronts)])]
    unnamed x9 -> x4, local copies, waits for them, and re-layouts: 7.84 us -> 6.84 us
  transfers between devices with their start and end apart: 5 -> 0, of which waited for: 4 -> 0; matrix products, arithmetic and copies ran while one was open for 12% -> 0% of each run, Pallas kernels for 0% -> 0%
where the time goes in v1:
time: 104 us
  Pallas kernels  94.7 us (91%)
  local copies, waits for them, and re-layouts  8.44 us (8%)
    pallas_call x1, Pallas kernels, body(): pl.pallas_call(fused_kernel, out_shape=(jax.ShapeDtypeStruct((upd, order)...  94.7 us
    unnamed x4, local copies, waits for them, and re-layouts  6.84 us

profile of v1, /device:TPU:0, one launch (start us, length us, event | category | flops | bytes accessed | tf_op | source)
XLA Modules:
  0.0 103.8 jit_solution(18249623463012908028)
XLA Ops:
  0.6 1.6 %reshape.7.maps_ref = s32[32,576]{1,0:T(8,128)} reshape(s32[8,2304]{1,0:T(8,128)} %param.7) | data formatting | bytes 147456 | tf_op jit(solution)/shard_map/reshape | solution.py:239
  2.2 94.7 %shard_map.59 = (f32[576,768]{1,0:T(8,128)}, f32[768,768]{1,0:T(8,128)}) custom-call(s32[32,576]{1,0:T(8,128)} %reshape.7.maps_ref, f32[192,768]{1,0:T(8,128)} %bitcast.9, f32[576,768]{1,0:T(8,128)} %bitcast.8, f32[576,2304]{1,0:T(8,128)} %bitcast.5), custom_call_target="tpu_custom_call" | custom-call | tf_op jit(solution)/shard_map/pallas_call | solution.py:241
  96.9 0.0 copy-start
  96.9 5.6 %copy.6 = f32[768,1,768]{2,1,0:T(1,128)} copy(f32[768,1,768]{2,0,1:T(8,128)} %bitcast.6) | data formatting | bytes 4718592
  102.6 0.0 copy-done
  102.6 1.2 %copy.8 = f32[1,576,768]{2,1,0:T(8,128)} copy(f32[1,576,768]{2,1,0:T(8,128)S(1)} %bitcast.7) | data formatting | bytes 3538944
Async XLA Ops:
  96.9 5.6 %copy-start = (f32[576,768]{1,0:T(8,128)S(1)}, f32[576,768]{1,0:T(8,128)}, u32[]{:S(2)}) copy-start(f32[576,768]{1,0:T(8,128)} %get-tuple-element.4) | copy-start | bytes 5308420

commit v2 on v1

--- a/solution.py
+++ b/solution.py
@@ -22,7 +22,9 @@
 
 
 def dot3(a, b):
-    return dot_t(a[0], b[0]) + (dot_t(a[0], b[1]) + dot_t(a[1], b[0]))
+    return dot_t(
+        jnp.concatenate([a[0], a[0], a[1]], axis=1), jnp.concatenate([b[0], b[1], b[0]], axis=1)
+    )
 
 
 def inverse_factor(block):
@@ -69,7 +71,8 @@
 
 def fused_kernel(
     maps_ref, pivot_ref, coupling_ref, trailing_ref, factor_ref, front_ref,
-    raw, work, rows_left, panels, old_flat, old, outgoing, incoming,
+    raw, work, rows_left, panels, pend, pend_own, old_flat, old,
+    outgoing, outgoing_tail, incoming, incoming_tail,
     old_sem, piv_send, piv_recv, pan_send, pan_recv, upd_send, upd_recv,
 ):
     order = pivot_ref.shape[1]
@@ -148,13 +151,23 @@
         old[b] = old_flat[:, b * upd : (b + 1) * upd]
     relay(pivot_copy, 0)
 
+    pend[...] = jnp.zeros_like(pend)
+    pend_own[...] = jnp.zeros_like(pend_own)
     row_id = lax.broadcasted_iota(jnp.int32, (order, BLK), 0)
 
     def step(k, carry):
         at = cols(k)
         pivot_copy(1, k, mate, mate).wait_recv()
         pivot_copy(2, k, mate_across, mate).wait_recv()
-        inverse = halves(inverse_factor(raw[at, at] + work[at, at]))
+        corner = (pend[0, at, :], pend[1, at, :])
+        inverse = halves(inverse_factor(raw[at, at] + (work[at, at] - dot3(corner, corner))))
+        last = (pend[0], pend[1])
+        last_own = (pend_own[0], pend_own[1])
+        for c in range(0, order, 256):
+            cs = slice(c, c + 256)
+            part = (last[0][cs], last[1][cs])
+            work[:, cs] = work[:, cs] - dot3(last, part)
+            rows_left[:, cs] = rows_left[:, cs] - dot3(last_own, part)
 
         @pl.when(k + 1 < blocks)
         def _():
@@ -166,57 +179,103 @@
 
         solved = dot3(halves(rows_left[:, at]), inverse)
         factor_ref[:, at] = solved
-        panels[me, :, at] = solved.astype(jnp.bfloat16)
+        solved = halves(solved)
+        panels[me, :, at] = solved[0]
         panel_copy(0, k, me, across).start()
         panel_copy(1, k, me, mate).start()
         column = jnp.where(row_id >= k * BLK, raw[:, at] + work[:, at], 0.0)
         panel = halves(dot3(halves(column), inverse))
-        solved = halves(solved)
-        for c in range(0, order, 256):
-            cs = slice(c, c + 256)
-            part = (panel[0][cs], panel[1][cs])
-            work[:, cs] = work[:, cs] - dot3(panel, part)
-            rows_left[:, cs] = rows_left[:, cs] - dot3(solved, part)
+        for half in range(2):
+            pend[half] = panel[half]
+            pend_own[half] = solved[half]
         return carry
 
     lax.fori_loop(0, blocks, step, 0)
-    relay(panel_copy, blocks - 1)
-    for k in range(blocks):
+
+    most = order - BLK
+
+    def early(apart):
+        there = relative(apart)
+        old[there] = old[there] - dot_t(panels[me, :, :most], panels[there, :, :most])
+
+    for k in range(blocks - 1):
         panel_copy(1, k, mate, mate).wait_recv()
         panel_copy(2, k, mate_across, mate).wait_recv()
-
-    def update_copy(apart):
-        return pltpu.make_async_remote_copy(
-            src_ref=outgoing.at[apart],
-            dst_ref=incoming.at[apart - 1],
-            send_sem=upd_send.at[apart],
-            recv_sem=upd_recv.at[apart],
-            device_id={"front": sib_child(apart)},
-            device_id_type=MESH,
-        )
+    early(3)
+    relay(panel_copy, blocks - 1)
+    for apart in (1, 2, 0):
+        early(apart)
+    panel_copy(1, blocks - 1, mate, mate).wait_recv()
+    panel_copy(2, blocks - 1, mate_across, mate).wait_recv()
+
+    full = upd // BLK * BLK
+    folds = BLK // (upd - full)
+    fold_rows = upd // folds
+    fold = [slice(f * fold_rows, (f + 1) * fold_rows) for f in range(folds)]
+
+    def update_copies(apart):
+        return [
+            pltpu.make_async_remote_copy(
+                src_ref=source.at[apart],
+                dst_ref=target.at[apart - 1],
+                send_sem=upd_send.at[which, apart],
+                recv_sem=upd_recv.at[which, apart],
+                device_id={"front": sib_child(apart)},
+                device_id_type=MESH,
+            )
+            for which, (source, target) in enumerate(
+                ((outgoing, incoming), (outgoing_tail, incoming_tail))
+            )
+        ]
 
     for apart in (3, 1, 2, 0):
         there = relative(apart)
-        outgoing[apart] = (old[there] - dot_t(panels[me], panels[there])).astype(jnp.bfloat16)
+        piece = old[there] - dot_t(panels[me, :, most:], panels[there, :, most:])
+        outgoing[apart] = piece[:, :full].astype(jnp.bfloat16)
+        outgoing_tail[apart] = jnp.concatenate([piece[f, full:] for f in fold], axis=1).astype(
+            jnp.bfloat16
+        )
         if apart:
-            update_copy(apart).start()
+            for copy in update_copies(apart):
+                copy.start()
 
     row_count, col_count = front_ref.shape
     target_rows = lax.broadcasted_iota(jnp.int32, (row_count, upd), 0)
     target_cols = lax.broadcasted_iota(jnp.int32, (col_count, upd), 0)
+    tail_lane = lax.broadcasted_iota(jnp.int32, (col_count, BLK), 1)
+
+    def one_hot(targets, sources):
+        return jnp.where(targets == sources, 1.0, 0.0).astype(jnp.bfloat16)
+
+    def map_block(child_map, which):
+        found = jnp.zeros((1, upd), jnp.int32)
+        for b in range(SIBLINGS):
+            found = jnp.where(which == b, child_map[:, b * upd : (b + 1) * upd], found)
+        return found
+
     for apart in (0, 1, 2, 3):
+        child_map = maps_ref[pl.ds(sib_child(apart), 1), :]
+        rows_map = map_block(child_map, me) - me * row_count
+        cols_map = map_block(child_map, sibling) - sibling * col_count
+        tail_map = jnp.concatenate([cols_map[:, full:]] * folds, axis=1)
+        row_hot = one_hot(target_rows, rows_map)
+        col_hot = one_hot(target_cols[:, :full], cols_map[:, :full])
+        tail_hot = [
+            one_hot(
+                jnp.where(lax.div(tail_lane, upd - full) == f, target_cols[:, :BLK], -1), tail_map
+            )
+            for f in range(folds)
+        ]
         if apart:
-            update_copy(apart).wait_recv()
-            value = incoming[apart - 1]
+            for copy in update_copies(apart):
+                copy.wait_recv()
+            value, tail = incoming[apart - 1], incoming_tail[apart - 1]
         else:
-            value = outgoing[0]
-        base = sib_child(apart) * SIBLINGS
-        rows_map = maps_ref[pl.ds(base + me, 1), :] - me * row_count
-        cols_map = maps_ref[pl.ds(base + sibling, 1), :] - sibling * col_count
-        row_hot = jnp.where(target_rows == rows_map, 1.0, 0.0).astype(jnp.bfloat16)
-        col_hot = jnp.where(target_cols == cols_map, 1.0, 0.0).astype(jnp.bfloat16)
-        moved = dot_t(value, col_hot).astype(jnp.bfloat16)
-        placed = jnp.dot(row_hot, moved, preferred_element_type=jnp.float32)
+            value, tail = outgoing[0], outgoing_tail[0]
+        moved = dot_t(value, col_hot) + jnp.concatenate(
+            [dot_t(tail, hot) for hot in tail_hot], axis=0
+        )
+        placed = jnp.dot(row_hot, moved.astype(jnp.bfloat16), preferred_element_type=jnp.float32)
         if apart:
             front_ref[...] += placed
         else:
@@ -227,7 +286,8 @@
             pivot_copy(kind, k, owner, peer).wait_send()
             panel_copy(kind, k, owner, peer).wait_send()
     for apart in (1, 2, 3):
-        update_copy(apart).wait_send()
+        for copy in update_copies(apart):
+            copy.wait_send()
 
 
 def body(pivot_block, coupling_rows, trailing_block, index_map):
@@ -236,7 +296,8 @@
     upd, upd_all = trailing_block.shape[1:]
     blocks = order // BLK
     row_count, col_count = PO // pairs, PO // SIBLINGS
-    maps = index_map.reshape(-1, upd)
+    full = upd // BLK * BLK
+    folded = upd * (upd - full) // BLK
     vmem = pl.BlockSpec(memory_space=pltpu.VMEM)
     factor, front = pl.pallas_call(
         fused_kernel,
@@ -251,22 +312,26 @@
             pltpu.VMEM((order, order), jnp.float32),
             pltpu.VMEM((upd, order), jnp.float32),
             pltpu.VMEM((pairs, upd, order), jnp.bfloat16),
+            pltpu.VMEM((2, order, BLK), jnp.bfloat16),
+            pltpu.VMEM((2, upd, BLK), jnp.bfloat16),
             pltpu.VMEM((upd, upd_all), jnp.float32),
             pltpu.VMEM((SIBLINGS, upd, upd), jnp.float32),
-            pltpu.VMEM((SIBLINGS, upd, upd), jnp.bfloat16),
-            pltpu.VMEM((SIBLINGS - 1, upd, upd), jnp.bfloat16),
+            pltpu.VMEM((SIBLINGS, upd, full), jnp.bfloat16),
+            pltpu.VMEM((SIBLINGS, folded, BLK), jnp.bfloat16),
+            pltpu.VMEM((SIBLINGS - 1, upd, full), jnp.bfloat16),
+            pltpu.VMEM((SIBLINGS - 1, folded, BLK), jnp.bfloat16),
             pltpu.SemaphoreType.DMA,
             pltpu.SemaphoreType.DMA((3, blocks)),
             pltpu.SemaphoreType.DMA((3, blocks)),
             pltpu.SemaphoreType.DMA((3, blocks)),
             pltpu.SemaphoreType.DMA((3, blocks)),
-            pltpu.SemaphoreType.DMA((SIBLINGS,)),
-            pltpu.SemaphoreType.DMA((SIBLINGS,)),
+            pltpu.SemaphoreType.DMA((2, SIBLINGS)),
+            pltpu.SemaphoreType.DMA((2, SIBLINGS)),
         ],
         compiler_params=pltpu.CompilerParams(
             collective_id=0, has_side_effects=True, vmem_limit_bytes=56 * 2**20
         ),
-    )(maps, pivot_block[0], coupling_rows[0], trailing_block[0])
+    )(index_map, pivot_block[0], coupling_rows[0], trailing_block[0])
     return (factor[None, :, :], front[:, None, :])
 
 

time: 104 us -> 95.9 us (0.922)
  Pallas kernels: 94.7 us -> 88.3 us
  local copies, waits for them, and re-layouts: 8.44 us -> 6.84 us
    pallas_call x1, Pallas kernels: 94.7 us -> 88.3 us  [body(): pl.pallas_call(fused_kernel, out_shape=(jax.ShapeDtypeStruct((upd, order)...]
    reshape x1 -> x0, local copies, waits for them, and re-layouts: 1.61 us -> none  [body(): maps = index_map.reshape(-1, upd)]
where the time goes in v2:
time: 95.9 us; the launch traced here: 95.8 us
  Pallas kernels  88.3 us (92%)
  local copies, waits for them, and re-layouts  6.84 us (7%)
    pallas_call x1, Pallas kernels, body(): pl.pallas_call(fused_kernel, out_shape=(jax.ShapeDtypeStruct((upd, order)...  88.3 us
    unnamed x4, local copies, waits for them, and re-layouts  6.84 us

profile of v2, /device:TPU:0, one launch (start us, length us, event | category | flops | bytes accessed | tf_op | source)
XLA Modules:
  0.0 95.8 jit_solution(1919718044964400343)
XLA Ops:
  0.6 88.3 %shard_map.59 = (f32[576,768]{1,0:T(8,128)}, f32[768,768]{1,0:T(8,128)}) custom-call(s32[8,2304]{1,0:T(8,128)} %maps_ref.1, f32[192,768]{1,0:T(8,128)} %bitcast.9, f32[576,768]{1,0:T(8,128)} %bitcast.7, f32[576,2304]{1,0:T(8,128)} %bitcast.5), custom_call_target="tpu_custom_call" | custom-call | tf_op jit(solution)/shard_map/pallas_call | solution.py:302
  88.9 0.0 copy-start
  89.0 5.6 %copy.6 = f32[768,1,768]{2,1,0:T(1,128)} copy(f32[768,1,768]{2,0,1:T(8,128)} %bitcast.6) | data formatting | bytes 4718592
  94.6 0.0 copy-done
  94.6 1.2 %copy.8 = f32[1,576,768]{2,1,0:T(8,128)} copy(f32[1,576,768]{2,1,0:T(8,128)S(1)} %bitcast.8) | data formatting | bytes 3538944
Async XLA Ops:
  88.9 5.6 %copy-start = (f32[576,768]{1,0:T(8,128)S(1)}, f32[576,768]{1,0:T(8,128)}, u32[]{:S(2)}) copy-start(f32[576,768]{1,0:T(8,128)} %get-tuple-element.4) | copy-start | bytes 5308420

commit v3 on v2

--- a/solution.py
+++ b/solution.py
@@ -31,7 +31,12 @@
     size = block.shape[0]
     sub = lax.broadcasted_iota(jnp.int32, (SUB, size), 0)
     lane = lax.broadcasted_iota(jnp.int32, (SUB, size), 1)
-    rest = block
+    row_id = lax.broadcasted_iota(jnp.int32, (size, size), 0)
+    col_id = lax.broadcasted_iota(jnp.int32, (size, size), 1)
+    diagonal = jnp.where(row_id == col_id, block, 0.0)
+    across = lax.rsqrt(jnp.sum(diagonal, axis=0, keepdims=True))
+    down = lax.rsqrt(jnp.sum(diagonal, axis=1, keepdims=True))
+    rest = block * across * down
     done = []
     for start in range(0, size, SUB):
         rows = size - start
@@ -47,26 +52,37 @@
             below = rest[SUB:]
             low = [c[SUB:] for c in cols]
         scale = jnp.ones((SUB, size), jnp.float32)
-        for t in range(SUB):
-            pivot = top[t][t : t + 1, :]
-            recip = 1.0 / pivot
-            scale = jnp.where(sub == t, lax.rsqrt(pivot), scale)
-            for j in range(t + 1, SUB):
-                mult = top[j][t : t + 1, :] * recip
-                top[j] = top[j] - top[t] * mult
+        for t in range(0, SUB, 2):
+            first, second = top[t], top[t + 1]
+            a, b, c = first[t : t + 1], second[t : t + 1], second[t + 1 : t + 2]
+            det = a * c - b * b
+            recip = 1.0 / det
+            recip_a = 1.0 / a
+            scale = jnp.where(sub == t, lax.rsqrt(a), scale)
+            scale = jnp.where(sub == t + 1, lax.rsqrt(det * recip_a), scale)
+            a, b, c = a * recip, b * recip, c * recip
+            ratio = second[t : t + 1] * recip_a
+
+            def pair_of(value):
+                g, h = value[t : t + 1], value[t + 1 : t + 2]
+                return c * g - b * h, a * h - b * g
+
+            for j in range(t + 2, SUB):
+                one, two = pair_of(top[j])
+                top[j] = top[j] - (first * one + second * two)
                 if more:
-                    low[j] = low[j] - low[t] * mult
-            row = slab[t : t + 1, :] * recip
-            slab = slab - jnp.where(sub > t, top[t], 0.0) * row
+                    low[j] = low[j] - (low[t] * one + low[t + 1] * two)
+            one, two = pair_of(slab)
+            upper = slab[t : t + 1]
+            later = sub > t + 1
+            change = jnp.where(later, first, 0.0) * one + jnp.where(later, second, 0.0) * two
+            slab = slab - jnp.where(sub == t + 1, ratio * upper, change)
             if more:
-                below = below - low[t] * row
+                below = below - (low[t] * one + low[t + 1] * two)
         done.append(slab * scale)
         if more:
             rest = below
-    whole = jnp.concatenate(done, axis=0)
-    row_id = lax.broadcasted_iota(jnp.int32, (size, size), 0)
-    col_id = lax.broadcasted_iota(jnp.int32, (size, size), 1)
-    return jnp.where(col_id <= row_id, whole, 0.0)
+    return jnp.where(col_id <= row_id, jnp.concatenate(done, axis=0) * across, 0.0)
 
 
 def fused_kernel(

time: 95.9 us -> 96.8 us (level)
  no operation moved by 1% of the time
where the time goes in v3:
time: 96.8 us; the launch traced here: 96.6 us
  Pallas kernels  89.1 us (92%)
  local copies, waits for them, and re-layouts  6.84 us (7%)
    pallas_call x1, Pallas kernels, body(): pl.pallas_call(fused_kernel, out_shape=(jax.ShapeDtypeStruct((upd, order)...  89.1 us
    unnamed x4, local copies, waits for them, and re-layouts  6.84 us

profile of v3, /device:TPU:0, one launch (start us, length us, event | category | flops | bytes accessed | tf_op | source)
XLA Modules:
  0.0 96.6 jit_solution(14409680489097307703)
XLA Ops:
  0.6 89.1 %shard_map.59 = (f32[576,768]{1,0:T(8,128)}, f32[768,768]{1,0:T(8,128)}) custom-call(s32[8,2304]{1,0:T(8,128)} %maps_ref.1, f32[192,768]{1,0:T(8,128)} %bitcast.9, f32[576,768]{1,0:T(8,128)} %bitcast.7, f32[576,2304]{1,0:T(8,128)} %bitcast.5), custom_call_target="tpu_custom_call" | custom-call | tf_op jit(solution)/shard_map/pallas_call | solution.py:318
  89.8 0.0 copy-start
  89.8 5.6 %copy.6 = f32[768,1,768]{2,1,0:T(1,128)} copy(f32[768,1,768]{2,0,1:T(8,128)} %bitcast.6) | data formatting | bytes 4718592
  95.4 0.0 copy-done
  95.4 1.2 %copy.8 = f32[1,576,768]{2,1,0:T(8,128)} copy(f32[1,576,768]{2,1,0:T(8,128)S(1)} %bitcast.8) | data formatting | bytes 3538944
Async XLA Ops:
  89.8 5.6 %copy-start = (f32[576,768]{1,0:T(8,128)S(1)}, f32[576,768]{1,0:T(8,128)}, u32[]{:S(2)}) copy-start(f32[576,768]{1,0:T(8,128)} %get-tuple-element.4) | copy-start | bytes 5308420

commit v4 on v2

--- a/solution.py
+++ b/solution.py
@@ -70,10 +70,10 @@
 
 
 def fused_kernel(
-    maps_ref, pivot_ref, coupling_ref, trailing_ref, factor_ref, front_ref,
-    raw, work, rows_left, panels, pend, pend_own, old_flat, old,
+    maps_ref, pivot_ref, coupling_ref, trailing_ref, factor_out, front_ref,
+    factor_ref, total, raw, work, rows_left, panels, pend, pend_own, old_flat, old,
     outgoing, outgoing_tail, incoming, incoming_tail,
-    old_sem, piv_send, piv_recv, pan_send, pan_recv, upd_send, upd_recv,
+    io_sem, piv_send, piv_recv, pan_send, pan_recv, upd_send, upd_recv,
 ):
     order = pivot_ref.shape[1]
     own_rows = pivot_ref.shape[0]
@@ -103,7 +103,9 @@
         pl.semaphore_signal(
             barrier, inc=1, device_id={"front": sib_child(apart)}, device_id_type=MESH
         )
-    load_old = pltpu.make_async_copy(trailing_ref, old_flat, old_sem)
+    load_rows = pltpu.make_async_copy(coupling_ref, rows_left, io_sem.at[0])
+    load_rows.start()
+    load_old = pltpu.make_async_copy(trailing_ref, old_flat, io_sem.at[1])
     load_old.start()
     pl.semaphore_wait(barrier, 5)
 
@@ -144,8 +146,8 @@
         pivot_copy(1, k, me, mate).start()
 
     raw[pivot_rows(me), :] = pivot_ref[...]
-    rows_left[...] = coupling_ref[...]
     work[...] = jnp.zeros_like(work)
+    load_rows.wait()
     load_old.wait()
     for b in range(SIBLINGS):
         old[b] = old_flat[:, b * upd : (b + 1) * upd]
@@ -173,7 +175,11 @@
         def _():
             relay(pivot_copy, k + 1)
 
-        @pl.when(k > 0)
+        @pl.when(k == 2)
+        def _():
+            relay(panel_copy, 0)
+
+        @pl.when(k >= 2)
         def _():
             relay(panel_copy, k - 1)
 
@@ -191,6 +197,8 @@
         return carry
 
     lax.fori_loop(0, blocks, step, 0)
+    store_factor = pltpu.make_async_copy(factor_ref, factor_out, io_sem.at[2])
+    store_factor.start()
 
     most = order - BLK
 
@@ -239,7 +247,7 @@
             for copy in update_copies(apart):
                 copy.start()
 
-    row_count, col_count = front_ref.shape
+    row_count, col_count = total.shape
     target_rows = lax.broadcasted_iota(jnp.int32, (row_count, upd), 0)
     target_cols = lax.broadcasted_iota(jnp.int32, (col_count, upd), 0)
     tail_lane = lax.broadcasted_iota(jnp.int32, (col_count, BLK), 1)
@@ -276,10 +284,12 @@
             [dot_t(tail, hot) for hot in tail_hot], axis=0
         )
         placed = jnp.dot(row_hot, moved.astype(jnp.bfloat16), preferred_element_type=jnp.float32)
-        if apart:
-            front_ref[...] += placed
+        if apart == 0:
+            total[...] = placed
+        elif apart < SIBLINGS - 1:
+            total[...] += placed
         else:
-            front_ref[...] = placed
+            front_ref[:, 0, :] = total[...] + placed
 
     for k in range(blocks):
         for kind, owner, peer in ((0, me, across), (1, me, mate), (2, across, mate)):
@@ -288,6 +298,7 @@
     for apart in (1, 2, 3):
         for copy in update_copies(apart):
             copy.wait_send()
+    store_factor.wait()
 
 
 def body(pivot_block, coupling_rows, trailing_block, index_map):
@@ -299,15 +310,18 @@
     full = upd // BLK * BLK
     folded = upd * (upd - full) // BLK
     vmem = pl.BlockSpec(memory_space=pltpu.VMEM)
+    hbm = pl.BlockSpec(memory_space=pl.ANY)
     factor, front = pl.pallas_call(
         fused_kernel,
         out_shape=(
             jax.ShapeDtypeStruct((upd, order), jnp.float32),
-            jax.ShapeDtypeStruct((row_count, col_count), jnp.float32),
+            jax.ShapeDtypeStruct((row_count, 1, col_count), jnp.float32),
         ),
-        in_specs=[vmem, vmem, vmem, pl.BlockSpec(memory_space=pl.ANY)],
-        out_specs=[vmem, vmem],
+        in_specs=[vmem, vmem, hbm, hbm],
+        out_specs=[hbm, vmem],
         scratch_shapes=[
+            pltpu.VMEM((upd, order), jnp.float32),
+            pltpu.VMEM((row_count, col_count), jnp.float32),
             pltpu.VMEM((order, order), jnp.float32),
             pltpu.VMEM((order, order), jnp.float32),
             pltpu.VMEM((upd, order), jnp.float32),
@@ -320,7 +334,7 @@
             pltpu.VMEM((SIBLINGS, folded, BLK), jnp.bfloat16),
             pltpu.VMEM((SIBLINGS - 1, upd, full), jnp.bfloat16),
             pltpu.VMEM((SIBLINGS - 1, folded, BLK), jnp.bfloat16),
-            pltpu.SemaphoreType.DMA,
+            pltpu.SemaphoreType.DMA((3,)),
             pltpu.SemaphoreType.DMA((3, blocks)),
             pltpu.SemaphoreType.DMA((3, blocks)),
             pltpu.SemaphoreType.DMA((3, blocks)),
@@ -332,7 +346,7 @@
             collective_id=0, has_side_effects=True, vmem_limit_bytes=56 * 2**20
         ),
     )(index_map, pivot_block[0], coupling_rows[0], trailing_block[0])
-    return (factor[None, :, :], front[:, None, :])
+    return (factor[None, :, :], front)
 
 
 def solution(mesh):

time: 95.9 us -> 91.6 us (0.955)
  local copies, waits for them, and re-layouts: 6.84 us -> 4.36 us
  Pallas kernels: 88.3 us -> 86.5 us
    unnamed x4, local copies, waits for them, and re-layouts: 6.84 us -> 4.36 us
    pallas_call x1, Pallas kernels: 88.3 us -> 86.5 us  [body(): pl.pallas_call(fused_kernel, out_shape=(jax.ShapeDtypeStruct((upd, order)...]
where the time goes in v4:
time: 91.6 us; the launch traced here: 91.5 us
  Pallas kernels  86.5 us (94%)
  local copies, waits for them, and re-layouts  4.36 us (5%)
    pallas_call x1, Pallas kernels, body(): pl.pallas_call(fused_kernel, out_shape=(jax.ShapeDtypeStruct((upd, order)...  86.5 us
    unnamed x4, local copies, waits for them, and re-layouts  4.36 us

profile of v4, /device:TPU:0, one launch (start us, length us, event | category | flops | bytes accessed | tf_op | source)
XLA Modules:
  0.0 91.5 jit_solution(14663410515525785484)
XLA Ops:
  0.6 86.5 %shard_map.59 = (f32[576,768]{1,0:T(8,128)}, f32[768,1,768]{2,1,0:T(1,128)}) custom-call(s32[8,2304]{1,0:T(8,128)} %maps_ref.1, f32[192,768]{1,0:T(8,128)} %bitcast.7, f32[576,768]{1,0:T(8,128)} %bitcast.5, f32[576,2304]{1,0:T(8,128)} %bitcast.4), custom_call_target="tpu_custom_call" | custom-call | tf_op jit(solution)/shard_map/pallas_call | solution.py:314
  87.1 0.0 copy-start
  87.1 2.9 %copy.8 = f32[1,576,768]{2,1,0:T(8,128)} copy(f32[1,576,768]{2,1,0:T(8,128)} %bitcast.6) | data formatting | bytes 3538944
  90.1 0.0 copy-done
  90.1 1.4 %copy.9 = f32[768,1,768]{2,1,0:T(1,128)} copy(f32[768,1,768]{2,1,0:T(1,128)S(1)} %copy-done) | data formatting | bytes 4718592
Async XLA Ops:
  87.1 3.0 %copy-start = (f32[768,1,768]{2,1,0:T(1,128)S(1)}, f32[768,1,768]{2,1,0:T(1,128)}, u32[]{:S(2)}) copy-start(f32[768,1,768]{2,1,0:T(1,128)} %get-tuple-element.9) | copy-start | bytes 7077892

commit v5 on v4

--- a/solution.py
+++ b/solution.py
@@ -261,7 +261,7 @@
             found = jnp.where(which == b, child_map[:, b * upd : (b + 1) * upd], found)
         return found
 
-    for apart in (0, 1, 2, 3):
+    for apart in (0, 3, 1, 2):
         child_map = maps_ref[pl.ds(sib_child(apart), 1), :]
         rows_map = map_block(child_map, me) - me * row_count
         cols_map = map_block(child_map, sibling) - sibling * col_count
@@ -286,7 +286,7 @@
         placed = jnp.dot(row_hot, moved.astype(jnp.bfloat16), preferred_element_type=jnp.float32)
         if apart == 0:
             total[...] = placed
-        elif apart < SIBLINGS - 1:
+        elif apart != 2:
             total[...] += placed
         else:
             front_ref[:, 0, :] = total[...] + placed

time: 91.6 us -> 89.2 us (0.974)
  Pallas kernels: 86.5 us -> 84 us
    pallas_call x1, Pallas kernels: 86.5 us -> 84 us  [body(): pl.pallas_call(fused_kernel, out_shape=(jax.ShapeDtypeStruct((upd, order)...]
where the time goes in v5:
time: 89.2 us; the launch traced here: 89 us
  Pallas kernels  84 us (94%)
  local copies, waits for them, and re-layouts  4.36 us (5%)
    pallas_call x1, Pallas kernels, body(): pl.pallas_call(fused_kernel, out_shape=(jax.ShapeDtypeStruct((upd, order)...  84 us
    unnamed x4, local copies, waits for them, and re-layouts  4.36 us

profile of v5, /device:TPU:0, one launch (start us, length us, event | category | flops | bytes accessed | tf_op | source)
XLA Modules:
  0.0 89.0 jit_solution(6786650809142651613)
XLA Ops:
  0.6 84.0 %shard_map.59 = (f32[576,768]{1,0:T(8,128)}, f32[768,1,768]{2,1,0:T(1,128)}) custom-call(s32[8,2304]{1,0:T(8,128)} %maps_ref.1, f32[192,768]{1,0:T(8,128)} %bitcast.7, f32[576,768]{1,0:T(8,128)} %bitcast.5, f32[576,2304]{1,0:T(8,128)} %bitcast.4), custom_call_target="tpu_custom_call" | custom-call | tf_op jit(solution)/shard_map/pallas_call | solution.py:314
  84.6 0.0 copy-start
  84.7 2.9 %copy.8 = f32[1,576,768]{2,1,0:T(8,128)} copy(f32[1,576,768]{2,1,0:T(8,128)} %bitcast.6) | data formatting | bytes 3538944
  87.6 0.0 copy-done
  87.6 1.4 %copy.9 = f32[768,1,768]{2,1,0:T(1,128)} copy(f32[768,1,768]{2,1,0:T(1,128)S(1)} %copy-done) | data formatting | bytes 4718592
Async XLA Ops:
  84.6 3.0 %copy-start = (f32[768,1,768]{2,1,0:T(1,128)S(1)}, f32[768,1,768]{2,1,0:T(1,128)}, u32[]{:S(2)}) copy-start(f32[768,1,768]{2,1,0:T(1,128)} %get-tuple-element.9) | copy-start | bytes 7077892
